TPU v7x, 32 devices: a whole 2x2x4 slice. The times are simulated.
32 devices in a mesh: ens: 4 (over y, x), space: 8 (over z, core).
Axes of the slice: x: 2, y: 2, z: 4, core: 2. Of those that a mesh axis runs over, the one named last changes fastest.
Arguments:
- node_latent: bfloat16 [4, 2048, 512], P('ens', 'space'), may hold values from -6 to 6
- point_skip: bfloat16 [16384, 512], P('space'), may hold values from -6 to 6
- edge_index: int32 [3, 16384], P(None, 'space'), may hold values from 0 to 319
- edge_weight: float32 [3, 16384], P(None, 'space'), may hold values from 0.1 to 1
- w_in: bfloat16 [512, 512], replicated, may hold values from -0.25 to 0.25
- b_in: float32 [512], replicated, may hold values from -3 to 3
- readout_matrix: bfloat16 [10, 512], replicated, may hold values from -0.25 to 0.25
- output_bias: float32 [10], replicated, may hold values from -3 to 3
- truth: float32 [10, 16384], P(None, 'space'), may hold values from -6 to 6
Outputs:
- loss: float32 [], replicated
- grad_latent: float32 [4, 2048, 512], P('ens', 'space')
- grad_w_in: float32 [512, 512], replicated
- grad_b_in: float32 [512], replicated
- grad_w_out: float32 [10, 512], replicated
- grad_b_out: float32 [10], replicated
Inputs may be any that keep to these rules, and one draw needn't show every extreme that they name: edge_index[k, p] indexes the table of 320 mesh nodes of p's band: the last 32 nodes of the band before, the band's own 256, the first 32 of the band after.
All inputs are finite; a program needn't handle non-finite values.
Results may differ from a plain program's by a relative error of at most 0.019.
The roundings to bfloat16 on the way count: a program that leaves them out, or rounds other values in their place, can miss the bound.
Values may be sent and summed in bfloat16 or wider, within the bound.
A program may use at most 64 MiB of HBM per device.

v0:
```python
import math

import jax
import jax.numpy as jnp
from jax import lax
from jax.sharding import PartitionSpec as P

unbiasing_factor = 0.95


def extended_2(cells, sides, width):
    for axis, dim in sides:
        count = lax.axis_size(axis)
        ends = count - 1
        head = lax.slice_in_dim(cells, 0, width, axis=dim)
        tail = lax.slice_in_dim(cells, cells.shape[dim] - width, cells.shape[dim], axis=dim)
        cells = jnp.concatenate(
            [
                lax.ppermute(tail, axis, [(i, (i + 1) % count) for i in range(ends)]),
                cells,
                lax.ppermute(head, axis, [((i + 1) % count, i) for i in range(ends)]),
            ],
            axis=dim,
        )
    return cells


def shifted(value, axis, steps):
    count = lax.axis_size(axis)
    initial, last = (max(0, -steps), min(count, count - steps))
    return lax.ppermute(value, axis, [(source, source + steps) for source in range(initial, last)])


def mutual_gaps_between_draws(
    owned_entries_window, all_members, verifying_truth_state, per_draw_states
):
    spread_among_draws = owned_entries_window[:, None] - all_members[None]
    predicted_state_adjoint = jnp.sign(
        owned_entries_window - verifying_truth_state[None]
    ) / per_draw_states - unbiasing_factor / (per_draw_states * (per_draw_states - 1)) * jnp.sum(
        jnp.sign(spread_among_draws), axis=1
    )
    accumulated_total_so_far = jnp.sum(
        jnp.abs(owned_entries_window - verifying_truth_state[None])
    ) / per_draw_states - unbiasing_factor / (
        2.0 * per_draw_states * (per_draw_states - 1)
    ) * jnp.sum(
        jnp.abs(spread_among_draws)
    )
    return (predicted_state_adjoint, accumulated_total_so_far)


def per_device(
    node_latent, point_skip, edge_index, edge_weight, w_in, b_in, readout_matrix, output_bias, truth
):
    mem_dev, node_dev, feat_width = node_latent.shape
    rim_rows = node_dev // 8
    pts_dev = point_skip.shape[0]
    edge_count = edge_index.shape[0]
    var_count = truth.shape[0]
    per_draw_states = mem_dev * lax.axis_size("ens")
    points = pts_dev * lax.axis_size("space")
    adjoint_multiplier = 1.0 / math.sqrt(per_draw_states * points)
    table_len = node_dev + 2 * rim_rows
    extended = extended_2(node_latent, (("space", 1),), rim_rows)
    slots = jnp.arange(table_len, dtype=jnp.int32)
    edge_table = jnp.zeros((pts_dev, table_len), jnp.float32)
    for edge in range(edge_count):
        hits = (edge_index[edge][:, None] == slots[None, :]).astype(jnp.float32)
        edge_table = edge_table + edge_weight[edge][:, None] * hits
    gathered = jnp.einsum(
        "pq,mqc->mpc", edge_table, extended.astype(jnp.float32), precision=lax.Precision.HIGHEST
    )
    features = (point_skip.astype(jnp.float32)[None] + gathered).astype(jnp.bfloat16)
    preact = jnp.einsum("mpc,ch->mph", features, w_in, preferred_element_type=jnp.float32) + b_in
    inner_layer_response = jax.nn.silu(preact).astype(jnp.bfloat16)
    modelled_state_values = (
        jnp.einsum(
            "rfo,to->rtf", inner_layer_response, readout_matrix, preferred_element_type=jnp.float32
        )
        + output_bias[None, :, None]
    )
    all_members = lax.all_gather(modelled_state_values, "ens", axis=0, tiled=True)
    predicted_state_adjoint, accumulated_total_so_far = mutual_gaps_between_draws(
        modelled_state_values, all_members, truth, per_draw_states
    )
    readout_offset_adjoint = jnp.sum(predicted_state_adjoint, axis=(0, 2)) * adjoint_multiplier
    readout_matrix_adjoint = (
        jnp.einsum(
            "vsp,vpr->sr",
            predicted_state_adjoint,
            inner_layer_response.astype(jnp.float32),
            precision=lax.Precision.HIGHEST,
        )
        * adjoint_multiplier
    )
    inner_layer_adjoint = jnp.einsum(
        "hqs,qi->hsi",
        predicted_state_adjoint,
        readout_matrix.astype(jnp.float32),
        precision=lax.Precision.HIGHEST,
    )
    sigmoid_pre = jax.nn.sigmoid(preact)
    d_preact = (inner_layer_adjoint * sigmoid_pre * (1.0 + preact * (1.0 - sigmoid_pre))).astype(
        jnp.bfloat16
    )
    gb_in = jnp.sum(d_preact.astype(jnp.float32), axis=(0, 1)) * adjoint_multiplier
    gw_in = (
        jnp.einsum("mpc,mph->ch", features, d_preact, preferred_element_type=jnp.float32)
        * adjoint_multiplier
    )
    d_features = jnp.einsum("mph,ch->mpc", d_preact, w_in, preferred_element_type=jnp.float32)
    node_grad = jnp.einsum("pq,mpc->mqc", edge_table, d_features, precision=lax.Precision.HIGHEST)
    from_above = shifted(node_grad[:, :rim_rows], "space", -1)
    from_below = shifted(node_grad[:, node_dev + rim_rows :], "space", 1)
    inner = node_grad[:, rim_rows : rim_rows + node_dev]
    inner = inner.at[:, node_dev - rim_rows :].add(from_above)
    inner = inner.at[:, :rim_rows].add(from_below)
    gw_in, gb_in, readout_matrix_adjoint, readout_offset_adjoint, loss_sum = lax.psum(
        (gw_in, gb_in, readout_matrix_adjoint, readout_offset_adjoint, accumulated_total_so_far),
        ("ens", "space"),
    )
    loss = loss_sum / (points * var_count)
    return (loss, inner, gw_in, gb_in, readout_matrix_adjoint, readout_offset_adjoint)


def solution(mesh):
    return jax.shard_map(
        per_device,
        mesh=mesh,
        in_specs=(
            P("ens", "space", None),
            P("space", None),
            P(None, "space"),
            P(None, "space"),
            P(),
            P(),
            P(),
            P(),
            P(None, "space"),
        ),
        out_specs=(P(), P("ens", "space", None), P(), P(), P(), P()),
        check_vma=False,
    )
```

profile of v0, /device:TPU:0, one launch (start us, length us, event | category | flops | bytes accessed | tf_op | source)
XLA Modules:
  0.0 191.1 jit_solution(14424876587350103312)
XLA Ops:
  7.2 0.0 all-reduce.3.cloned.1.call-start
  7.2 0.9 fusion.29
  8.1 2.3 %collective-permute-start = (bf16[1,32,512]{2,1,0:T(8,128)(2,1)S(1)}, bf16[1,32,512]{2,1,0:T(8,128)(2,1)S(1)}, u32[]{:S(2)}, u32[]{:S(2)}) collective-permute-start(bf16[1,32,512]{2,1,0:T(8,128)(2,1)S(1)} %get-tuple-element.41), channel_id=1, source_target_pairs={{0,1},{1,2},{2,3},{3,4},{4,5},{5,6},{6,7},{8,9},{9,10},{10,11},{11... | collective-permute-start | bytes 98312 | tf_op jit(solution)/shard_map/ppermute | solution.py:19
  10.5 1.3 collective-permute-start.1
  11.8 0.9 fusion.30
  12.7 0.9 fusion.31
  13.6 2.9 %copy.16 = bf16[2048,512]{0,1:T(8,128)(2,1)S(1)} copy(bf16[2048,512]{1,0:T(8,128)(2,1)} %param.14) | data formatting | bytes 4194304 | tf_op args[1]
  16.5 5.9 %fusion.2 = bf16[2048,512]{0,1:T(8,128)(2,1)S(1)} fusion(bf16[2048,512]{0,1:T(8,128)(2,1)S(1)} %copy.16, f32[2048]{0:T(1024)S(1)} %bitcast.55, s32[2048]{0:T(1024)S(1)} %bitcast.49, f32[2048]{0:T(1024)S(1)} %bitcast.57, s32[2048]{0:T(1024)S(1)} %bitcast.51, f32[2048]{0:T(1024)S(1)} %bitcast.53, s32[2048]{0:T(1024)S(1)} %bitcast.47, ...), kind=kOutput, calls=%fused_computation.11 | convolution fusion | flops 4035903488 | bytes 4571136 | tf_op jit(solution)/shard_map/pq,mqc->mpc/dot_general | solution.py:71
  22.5 1.9 multiply_convert_fusion.1
  24.4 0.6 convolution_add_fusion
  25.1 11.9 %all-gather.1 = f32[4,10,2048]{2,1,0:T(8,128)S(1)} all-gather(f32[1,10,2048]{2,1,0:T(8,128)S(1)} %bitcast.45), channel_id=2, replica_groups=mesh['ens'=4,'space'=8] {'ens'}, dimensions={0}, use_global_device_ids=true | all-gather | bytes 409600 | tf_op jit(solution)/shard_map/all_gather | solution.py:83
  36.9 0.8 sign_reduce_fusion
  37.7 0.7 fusion.27
  38.4 0.9 convolution_multiply_fusion.1
  39.3 3.3 %convert_reduce_fusion = (f32[512]{0:T(512)S(1)}, bf16[2048,512]{1,0:T(8,128)(2,1)S(1)}) fusion(f32[2048,512]{1,0:T(8,128)S(1)} %get-tuple-element.50, f32[512]{0:T(512)S(1)} %copy-done.6, f32[10,2048]{1,0:T(8,128)S(1)} %get-tuple-element.37, bf16[10,512]{1,0:T(8,128)(2,1)S(1)} %copy-done.3), kind=kOutput, calls=%fused_computation.2 | convolution fusion | flops 138411520 | bytes 6387712 | tf_op jit(solution)/shard_map/hqs,qi->hsi/dot_general | solution.py:97
  42.6 2.2 %convolution_multiply_fusion = f32[512,512]{1,0:T(8,128)} fusion(bf16[2048,512]{0,1:T(8,128)(2,1)S(1)} %fusion.2, bf16[2048,512]{1,0:T(8,128)(2,1)S(1)} %get-tuple-element.52), kind=kOutput, calls=%fused_computation.27 | convolution fusion | flops 1074003968 | bytes 5242880 | tf_op jit(solution)/shard_map/mpc,mph->ch/dot_general | solution.py:109
  44.9 3.2 %fusion.32 = f32[2048,512]{1,0:T(8,128)} fusion(bf16[2048,512]{1,0:T(8,128)(2,1)S(1)} %get-tuple-element.52, bf16[512,512]{1,0:T(8,128)(2,1)S(1)} %copy-done), kind=kOutput, calls=%fused_computation.53 | convolution fusion | flops 1073741824 | bytes 6815744 | tf_op jit(solution)/shard_map/mph,ch->mpc/dot_general | solution.py:112
  48.1 0.0 all-reduce.3.cloned.1.call-update
  48.1 10.4 %fusion.17 = f32[1,320,512]{2,1,0:T(8,128)S(1)} fusion(f32[2048,512]{1,0:T(8,128)} %fusion.32, f32[2048]{0:T(1024)S(1)} %bitcast.56, s32[2048]{0:T(1024)S(1)} %bitcast.50, f32[2048]{0:T(1024)S(1)} %bitcast.58, s32[2048]{0:T(1024)S(1)} %bitcast.52, f32[2048]{0:T(1024)S(1)} %bitcast.54, s32[2048]{0:T(1024)S(1)} %bitcast.48), kind=kOutput, calls=%fused_computation.28 | convolution fusion | flops 4031774720 | bytes 4898816 | tf_op jit(solution)/shard_map/pq,mpc->mqc/dot_general | solution.py:113
  58.6 1.3 collective-permute-start.2
  61.2 3.0 %collective-permute-start.3 = (f32[1,32,512]{2,1,0:T(8,128)S(1)}, f32[1,32,512]{2,1,0:T(8,128)S(1)}, u32[]{:S(2)}, u32[]{:S(2)}) collective-permute-start(f32[1,32,512]{2,1,0:T(8,128)S(1)} %get-tuple-element.38), channel_id=1, source_target_pairs={{0,1},{1,2},{2,3},{3,4},{4,5},{5,6},{6,7},{8,9},{9,10},{10,11},{11... | collective-permute-start | bytes 196616 | tf_op jit(solution)/shard_map/ppermute | solution.py:31
  64.3 43.6 %all-reduce = (f32[]{:T(128)}, f32[512]{0:T(512)}, f32[10,512]{1,0:T(8,128)}, f32[10]{0:T(128)}) all-reduce(f32[]{:T(128)S(6)} %sub.28, f32[512]{0:T(512)S(1)} %broadcast_multiply_fusion, f32[10,512]{1,0:T(8,128)S(1)} %convolution_multiply_fusion.1, f32[10]{0:T(128)S(1)} %broadcast_multiply_fusion.1), channel_id=1, replica_groups=mesh['ens'=4,'space'=8] {'ens','space'}, use_global_device_ids=true, to_apply=%region_2.3 | all-reduce | flops 5643 | bytes 45144 | tf_op jit(solution)/shard_map/psum | solution.py:119
  108.6 72.3 %all-reduce.3.cloned.1.call-done = f32[512,512]{1,0:T(8,128)} async-done(((f32[512,512]{1,0:T(8,128)}), f32[512,512]{1,0:T(8,128)}) %all-reduce.3.cloned.1.call-update) | async-done | bytes 1048592 | tf_op jit(solution)/shard_map/psum | solution.py:119
  180.9 2.3 %copy.20 = f32[512,512]{1,0:T(8,128)} copy(f32[512,512]{1,0:T(8,128)} %all-reduce.3.cloned.1.call-done) | data formatting | bytes 2097152
  (24 shorter events, 0.1 us)
Async XLA Ops:
  7.2 15.3 %copy-start = (bf16[512,512]{1,0:T(8,128)(2,1)S(1)}, bf16[512,512]{1,0:T(8,128)(2,1)}, u32[]{:S(2)}) copy-start(bf16[512,512]{1,0:T(8,128)(2,1)} %param.17) | copy-start | bytes 1572868
  7.2 9.3 %copy-start.4 = (bf16[1,256,512]{2,1,0:T(8,128)(2,1)S(1)}, bf16[1,256,512]{2,1,0:T(8,128)(2,1)}, u32[]{:S(2)}) copy-start(bf16[1,256,512]{2,1,0:T(8,128)(2,1)} %param.13) | copy-start | bytes 786436
  7.2 173.7 %all-reduce.3.cloned.1.call-start = ((), (), s32[]{:S(2)}) async-start(), calls=%async_computation | async-start | bytes 2097152 | tf_op jit(solution)/shard_map/psum | solution.py:119
  8.1 8.4 %collective-permute-start = (bf16[1,32,512]{2,1,0:T(8,128)(2,1)S(1)}, bf16[1,32,512]{2,1,0:T(8,128)(2,1)S(1)}, u32[]{:S(2)}, u32[]{:S(2)}) collective-permute-start(bf16[1,32,512]{2,1,0:T(8,128)(2,1)S(1)} %get-tuple-element.41), channel_id=1, source_target_pairs={{0,1},{1,2},{2,3},{3,4},{4,5},{5,6},{6,7},{8,9},{9,10},{10,11},{11... | collective-permute-start | bytes 98312 | tf_op jit(solution)/shard_map/ppermute | solution.py:19
  10.5 6.1 %collective-permute-start.1 = (bf16[1,32,512]{2,1,0:T(8,128)(2,1)S(1)}, bf16[1,32,512]{2,1,0:T(8,128)(2,1)S(1)}, u32[]{:S(2)}, u32[]{:S(2)}) collective-permute-start(bf16[1,32,512]{2,1,0:T(8,128)(2,1)S(1)} %get-tuple-element.42), channel_id=1, source_target_pairs={{1,0},{2,1},{3,2},{4,3},{5,4},{6,5},{7,6},{9,8},{10,9},{11,10},{12... | collective-permute-start | bytes 98312 | tf_op jit(solution)/shard_map/ppermute | solution.py:21
  16.5 5.9 %copy-start.6 = (f32[512]{0:T(512)S(1)}, f32[512]{0:T(512)}, u32[]{:S(2)}) copy-start(f32[512]{0:T(512)} %param.18) | copy-start | bytes 6148
  22.5 1.9 %copy-start.3 = (bf16[10,512]{1,0:T(8,128)(2,1)S(1)}, bf16[10,512]{1,0:T(8,128)(2,1)}, u32[]{:S(2)}) copy-start(bf16[10,512]{1,0:T(8,128)(2,1)} %param.19) | copy-start | bytes 30724
  22.5 1.9 %copy-start.5 = (f32[10]{0:T(128)S(1)}, f32[10]{0:T(128)}, u32[]{:S(2)}) copy-start(f32[10]{0:T(128)} %param.20) | copy-start | bytes 124
  24.4 13.3 %copy-start.2 = (f32[10,2048]{1,0:T(8,128)S(1)}, f32[10,2048]{1,0:T(8,128)}, u32[]{:S(2)}) copy-start(f32[10,2048]{1,0:T(8,128)} %param.21) | copy-start | bytes 245764
  58.6 49.9 %collective-permute-start.2 = (f32[1,32,512]{2,1,0:T(8,128)S(1)}, f32[1,32,512]{2,1,0:T(8,128)S(1)}, u32[]{:S(2)}, u32[]{:S(2)}) collective-permute-start(f32[1,32,512]{2,1,0:T(8,128)S(1)} %get-tuple-element.39), channel_id=1, source_target_pairs={{1,0},{2,1},{3,2},{4,3},{5,4},{6,5},{7,6},{9,8},{10,9},{11,10},{12... | collective-permute-start | bytes 196616 | tf_op jit(solution)/shard_map/ppermute | solution.py:31
  61.2 47.3 %collective-permute-start.3 = (f32[1,32,512]{2,1,0:T(8,128)S(1)}, f32[1,32,512]{2,1,0:T(8,128)S(1)}, u32[]{:S(2)}, u32[]{:S(2)}) collective-permute-start(f32[1,32,512]{2,1,0:T(8,128)S(1)} %get-tuple-element.38), channel_id=1, source_target_pairs={{0,1},{1,2},{2,3},{3,4},{4,5},{5,6},{6,7},{8,9},{9,10},{10,11},{11... | collective-permute-start | bytes 196616 | tf_op jit(solution)/shard_map/ppermute | solution.py:31
  108.6 74.5 %copy-start.1 = (f32[1,256,512]{2,1,0:T(8,128)}, f32[1,256,512]{2,1,0:T(8,128)S(1)}, u32[]{:S(2)}) copy-start(f32[1,256,512]{2,1,0:T(8,128)S(1)} %fusion.22) | copy-start | bytes 1572868
Sparse Core Ops, SparseCore 0:
  48.2 132.5 all-reduce.2
where the time goes:
time: 192 us; the launch traced here: 191 us
  waiting for transfers between devices  72.3 us (38%)
  blocking collectives  55.4 us (29%)
  matrix products  28.6 us (15%)
  between operations  17.4 us (9%)
  starting transfers between devices  8 us (4%)
  local copies, waits for them, and re-layouts  7.94 us (4%)
    psum x1, waiting for transfers between devices, per_device(): lax.psum((gw_in, gb_in, readout_matrix_adjoint, readout_offset_adjoint, a...  72.3 us
    psum x1, blocking collectives, per_device(): lax.psum((gw_in, gb_in, readout_matrix_adjoint, readout_offset_adjoint, a...  43.6 us
    all_gather x1, blocking collectives, per_device(): lax.all_gather(modelled_state_values, 'ens', axis=0, tiled=True)  11.9 us
    dot_general x1, matrix products, per_device(): jnp.einsum('pq,mpc->mqc', edge_table, d_features, precision=lax.Precision...  10.4 us
    dot_general x1, matrix products, per_device(): jnp.einsum('pq,mqc->mpc', edge_table, extended.astype(jnp.float32), preci...  5.9 us
    unnamed x16, local copies, waits for them, and re-layouts  5.24 us
    ppermute x2, starting transfers between devices, shifted(): lax.ppermute(value, axis, [(source, source + steps) for source in range(i...  4.33 us
  transfers between devices with their start and end apart: 5, of which 1 were waited for; matrix products, arithmetic and copies ran while one was open for 8% of the time, Pallas kernels for 0%

commit v1 on v0

v1 whole, which is shorter than its diff:
```python
import functools
import math

import jax
import jax.numpy as jnp
from jax import lax
from jax.experimental import pallas as pl
from jax.experimental.pallas import tpu as pltpu
from jax.sharding import PartitionSpec as P

UNBIASING = 0.95
F32 = jnp.float32
BF16 = jnp.bfloat16
NT = (((1,), (1,)), ((), ()))


def dot(a, b):
    return jnp.dot(a, b, preferred_element_type=F32)


def dot_nt(a, b):
    return lax.dot_general(a, b, NT, preferred_element_type=F32)


def sign(x):
    return jnp.where(x > 0, 1.0, 0.0) - jnp.where(x < 0, 1.0, 0.0)


def kernel(
    cfg,
    latent, skip_hbm, index, weight, w_in, b_in, readout, bias, truth,
    node_out, gw_out_ref, small_out,
    skip, ext, ext_t, table, w_t, feat, hid, slope, dpre, fc, fc_in,
    ro_pad, truth_pad, b_col, acc_bin, acc_bout, acc_loss, node_grad,
    rim_send, rim_recv, gw_send, sum_a, recv_a, send_b, sum_b, recv_b, send_c, recv_c, gout,
    small, small_a, small_b, small_c,
    local_sem, halo_s, halo_r, fc_s, fc_r, rim_s, rim_r, a_s, a_r, b_s, b_r, c_s, c_r,
    gc_s, gc_r, gb_s, gb_r, ga_s, ga_r, sa_s, sa_r, sb_s, sb_r, sc_s, sc_r,
):
    E, S, T, R = cfg
    Z = S // 2
    nodes, C = latent.shape
    H = w_in.shape[1]
    pts = skip.shape[0]
    K = index.shape[0]
    V = readout.shape[0]
    VP = ro_pad.shape[0]
    tiles = pts // T
    table_len = nodes + 2 * R
    e = lax.axis_index("ens")
    s = lax.axis_index("space")
    c = lax.rem(s, 2)
    z = lax.div(s, 2)
    partner = s + 1 - 2 * c
    far = s - 1 + 2 * c
    has_far = jnp.logical_and(far >= 0, far < S)

    skip_copy = pltpu.make_async_copy(skip_hbm, skip, local_sem)
    skip_copy.start()

    barrier = pltpu.get_barrier_semaphore()

    def greet(dev):
        pl.semaphore_signal(barrier, inc=1, device_id=dev, device_id_type=pl.DeviceIdType.MESH)

    def ens_peer(d):
        return lax.rem(e + d, E)

    def z_peer(d):
        return lax.rem(z + d, Z)

    greet((e, partner))
    for d in range(1, E):
        greet((ens_peer(d), s))
    for d in range(1, Z):
        greet((e, 2 * z_peer(d) + c))

    @pl.when(has_far)
    def _():
        greet((e, far))

    pl.semaphore_wait(barrier, E + Z - 1 + has_far.astype(jnp.int32))

    def remote(src, dst, ss, rs, dev):
        return pltpu.make_async_remote_copy(
            src_ref=src, dst_ref=dst, send_sem=ss, recv_sem=rs,
            device_id=dev, device_id_type=pl.DeviceIdType.MESH,
        )

    up = remote(latent.at[pl.ds(nodes - R, R)], ext.at[pl.ds(0, R)], halo_s.at[0], halo_r.at[0], (e, s + 1))
    down = remote(latent.at[pl.ds(0, R)], ext.at[pl.ds(R + nodes, R)], halo_s.at[1], halo_r.at[1], (e, s - 1))

    @pl.when(s < S - 1)
    def _():
        up.start()

    @pl.when(s > 0)
    def _():
        down.start()

    @pl.when(s == 0)
    def _():
        ext[pl.ds(0, R)] = jnp.zeros((R, C), BF16)

    @pl.when(s == S - 1)
    def _():
        ext[pl.ds(R + nodes, R)] = jnp.zeros((R, C), BF16)

    ext[pl.ds(R, nodes)] = latent[...]
    ext[pl.ds(table_len + R, nodes)] = latent[...]
    w_t[...] = jnp.transpose(w_in[...])
    b_col[...] = jnp.transpose(jnp.broadcast_to(b_in[...], (128, H)))
    ro_pad[...] = jnp.zeros_like(ro_pad)
    ro_pad[pl.ds(0, V)] = readout[...].astype(F32)
    truth_pad[...] = jnp.zeros_like(truth_pad)
    truth_pad[pl.ds(0, V)] = truth[...]
    acc_bin[...] = jnp.zeros_like(acc_bin)
    acc_bout[...] = jnp.zeros_like(acc_bout)
    acc_loss[...] = jnp.zeros_like(acc_loss)
    small[...] = jnp.zeros_like(small)
    ro = ro_pad[...].astype(BF16)
    ro_t = jnp.transpose(ro_pad[...]).astype(BF16)
    row_v = lax.broadcasted_iota(jnp.int32, (VP, 128), 0)
    lane_v = lax.broadcasted_iota(jnp.int32, (VP, 128), 1)
    bias_col = jnp.sum(
        jnp.where(row_v == lane_v, jnp.broadcast_to(bias[...], (VP, 128)), 0.0), axis=1, keepdims=True
    )

    def lanes(i):
        return pl.ds(pl.multiple_of(i * T, T), T)

    def make_table(i, carry):
        slot = lax.broadcasted_iota(jnp.int32, (table_len, T), 0)
        total = jnp.zeros((table_len, T), F32)
        for k in range(K):
            total = total + jnp.where(slot == index[pl.ds(k, 1), lanes(i)], weight[pl.ds(k, 1), lanes(i)], 0.0)
        high = total.astype(BF16)
        table[pl.ds(0, table_len), lanes(i)] = high
        table[pl.ds(table_len, table_len), lanes(i)] = (total - high.astype(F32)).astype(BF16)
        return carry

    lax.fori_loop(0, tiles, make_table, 0)
    skip_copy.wait()

    @pl.when(s < S - 1)
    def _():
        down.wait_recv()

    @pl.when(s > 0)
    def _():
        up.wait_recv()

    ext[pl.ds(table_len, R)] = ext[pl.ds(0, R)]
    ext[pl.ds(table_len + R + nodes, R)] = ext[pl.ds(R + nodes, R)]
    ext_t[...] = jnp.transpose(ext[...])

    units = 20.0 * E * (E - 1)
    from_truth = 20.0 * (E - 1)
    from_pair = 20.0 * UNBIASING

    def fc_copy(i, d):
        return remote(fc.at[i], fc_in.at[i, d - 1], fc_s.at[i, d - 1], fc_r.at[i, d - 1], (ens_peer(d), s))

    def forward(i, carry):
        at = lanes(i)
        skip_t = jnp.transpose(skip[at, :]).astype(F32)
        f = (skip_t + dot(ext_t[...], table[:, at])).astype(BF16)
        feat[:, at] = f
        col = b_col[...]
        pre = dot(w_t[...], f) + jnp.concatenate([col] * (T // 128), axis=1)
        sig = 1.0 / (1.0 + jnp.exp(-pre))
        h = pre * sig
        slope[:, at] = (sig + h * (1.0 - sig)) * (1.0 / units)
        hb = h.astype(BF16)
        hid[:, at] = hb
        fc[i] = (dot(ro, hb) + bias_col)[:V]
        for d in range(1, E):
            fc_copy(i, d).start()
        return carry

    lax.fori_loop(0, tiles, forward, 0)

    def backward(i, carry):
        at = lanes(i)
        for d in range(1, E):
            fc_copy(i, d).wait_recv()
        own = fc[i]
        gap = own - truth_pad[pl.ds(0, V), at]
        pairs = jnp.zeros_like(own)
        spread = jnp.zeros_like(own)
        for d in range(1, E):
            diff = own - fc_in[i, d - 1]
            pairs = pairs + sign(diff)
            spread = spread + jnp.abs(diff)
        adj = from_truth * sign(gap) - from_pair * pairs
        acc_bout[pl.ds(0, V)] += adj
        acc_loss[pl.ds(0, V)] += jnp.abs(gap) * (1.0 / E) - spread * (UNBIASING / (2.0 * E * (E - 1)))
        truth_pad[pl.ds(0, V), at] = adj
        g = truth_pad[:, at].astype(BF16)
        small[...] += dot_nt(g, hid[:, at])
        dp = (dot(ro_t, g) * slope[:, at]).astype(BF16)
        dpre[:, at] = dp
        dp32 = dp.astype(F32)
        part = dp32[:, 0:128]
        for j in range(1, T // 128):
            part = part + dp32[:, j * 128:(j + 1) * 128]
        acc_bin[...] += part
        return carry

    lax.fori_loop(0, tiles, backward, 0)

    row = lax.broadcasted_iota(jnp.int32, (VP, H), 0)
    lane = lax.broadcasted_iota(jnp.int32, (VP, H), 1)
    gb_in = jnp.sum(jnp.transpose(acc_bin[...]), axis=0, keepdims=True)
    gb_col = jnp.sum(acc_bout[...], axis=1, keepdims=True)
    loss_col = jnp.sum(acc_loss[...], axis=1, keepdims=True)
    tail = jnp.sum(
        jnp.where(lane == row, gb_col * (1.0 / units), 0.0) + jnp.where(lane == VP, loss_col, 0.0),
        axis=0, keepdims=True,
    )
    first = small[...] * (1.0 / units)
    first = first + jnp.where(row == V, gb_in, 0.0) + jnp.where(row == V + 1, tail, 0.0)
    small[...] = first
    copy_sa = remote(small, small_a, sa_s, sa_r, (e, partner))
    copy_sa.start()

    half = C // 2
    rows_b = half // E
    scatter_c = rows_b % (16 * Z) == 0
    rows_c = rows_b // Z if scatter_c else rows_b
    theirs = pl.multiple_of((1 - c) * half, half)
    mine = pl.multiple_of(c * half, half)
    gw_send[...] = dot_nt(feat[pl.ds(theirs, half), :], dpre[...]).astype(BF16)
    copy_a = remote(gw_send, recv_a, a_s, a_r, (e, partner))
    copy_a.start()

    copy_sa.wait()
    small[...] = small[...] + small_a[...]
    copies_sb = [remote(small, small_b.at[d - 1], sb_s.at[d - 1], sb_r.at[d - 1], (ens_peer(d), s)) for d in range(1, E)]
    for copy in copies_sb:
        copy.start()

    sum_a[...] = dot_nt(feat[pl.ds(mine, half), :], dpre[...])
    copy_a.wait()
    sum_a[...] = sum_a[...] + recv_a[...].astype(F32)
    send_b[...] = sum_a[...].astype(BF16)
    copies_b = [
        remote(
            send_b.at[pl.ds(pl.multiple_of(ens_peer(d) * rows_b, rows_b), rows_b)],
            recv_b.at[d - 1], b_s.at[d - 1], b_r.at[d - 1], (ens_peer(d), s),
        )
        for d in range(1, E)
    ]
    for copy in copies_b:
        copy.start()

    for copy in copies_sb:
        copy.wait()
    total = small[...]
    for d in range(1, E):
        total = total + small_b[d - 1]
    small[...] = total
    copies_sc = [remote(small, small_c.at[d - 1], sc_s.at[d - 1], sc_r.at[d - 1], (e, 2 * z_peer(d) + c)) for d in range(1, Z)]
    for copy in copies_sc:
        copy.start()

    node_grad[...] = jnp.zeros_like(node_grad)

    def spread_back(i, carry):
        at = lanes(i)
        df = dot(w_in[...], dpre[:, at]).astype(BF16)
        node_grad[...] += dot_nt(table[pl.ds(0, table_len), at], df)
        return carry

    lax.fori_loop(0, tiles, spread_back, 0)
    rim_send[0] = node_grad[pl.ds(R + nodes, R)].astype(BF16)
    rim_send[1] = node_grad[pl.ds(0, R)].astype(BF16)
    rim_up = remote(rim_send.at[0], rim_recv.at[0], rim_s.at[0], rim_r.at[0], (e, s + 1))
    rim_down = remote(rim_send.at[1], rim_recv.at[1], rim_s.at[1], rim_r.at[1], (e, s - 1))

    @pl.when(s < S - 1)
    def _():
        rim_up.start()

    @pl.when(s > 0)
    def _():
        rim_down.start()

    for copy in copies_b:
        copy.wait()
    total = sum_a[pl.ds(pl.multiple_of(e * rows_b, rows_b), rows_b)]
    for d in range(1, E):
        total = total + recv_b[d - 1].astype(F32)
    sum_b[...] = total
    send_c[...] = total.astype(BF16)
    copies_c = []
    for d in range(1, Z):
        if scatter_c:
            src = send_c.at[pl.ds(pl.multiple_of(z_peer(d) * rows_c, rows_c), rows_c)]
        else:
            src = send_c
        copies_c.append(remote(src, recv_c.at[d - 1], c_s.at[d - 1], c_r.at[d - 1], (e, 2 * z_peer(d) + c)))
    for copy in copies_c:
        copy.start()

    node_out[...] = node_grad[pl.ds(R, nodes)]

    @pl.when(s > 0)
    def _():
        rim_up.wait_recv()
        node_out[pl.ds(0, R)] += rim_recv[0].astype(F32)
        rim_down.wait_send()
        down.wait_send()

    @pl.when(s < S - 1)
    def _():
        rim_down.wait_recv()
        node_out[pl.ds(nodes - R, R)] += rim_recv[1].astype(F32)
        rim_up.wait_send()
        up.wait_send()

    def drain(i, carry):
        for d in range(1, E):
            fc_copy(i, d).wait_send()
        return carry

    lax.fori_loop(0, tiles, drain, 0)
    for copy in copies_sc:
        copy.wait()
    total = small[...]
    for d in range(1, Z):
        total = total + small_c[d - 1]
    small_out[...] = total

    base_b = pl.multiple_of(c * half + e * rows_b, rows_b)
    for copy in copies_c:
        copy.wait()
    if scatter_c:
        base_c = pl.multiple_of(base_b + z * rows_c, rows_c)
        total = sum_b[pl.ds(pl.multiple_of(z * rows_c, rows_c), rows_c)]
    else:
        base_c = base_b
        total = sum_b[...]
    for d in range(1, Z):
        total = total + recv_c[d - 1].astype(F32)
    gout[pl.ds(base_c, rows_c)] = total.astype(BF16)
    if scatter_c:
        piece = gout.at[pl.ds(base_c, rows_c)]
        copies_gc = [remote(piece, piece, gc_s.at[d - 1], gc_r.at[d - 1], (e, 2 * z_peer(d) + c)) for d in range(1, Z)]
        for copy in copies_gc:
            copy.start()
        for d in range(1, Z):
            copies_gc[d - 1].wait()
    piece = gout.at[pl.ds(base_b, rows_b)]
    copies_gb = [remote(piece, piece, gb_s.at[d - 1], gb_r.at[d - 1], (ens_peer(d), s)) for d in range(1, E)]
    for copy in copies_gb:
        copy.start()
    copies_ga = []
    for d in range(E):
        if d:
            copies_gb[d - 1].wait_recv()
        at = pl.multiple_of(c * half + lax.rem(e + E - d, E) * rows_b, rows_b)
        piece = gout.at[pl.ds(at, rows_b)]
        copy = remote(piece, piece, ga_s.at[d], ga_r.at[d], (e, partner))
        copy.start()
        copies_ga.append(copy)
    for copy in copies_gb:
        copy.wait_send()
    for copy in copies_ga:
        copy.wait()
    gw_out_ref[...] = gout[...]


def per_device(
    node_latent, point_skip, edge_index, edge_weight, w_in, b_in, readout_matrix, output_bias, truth
):
    members, nodes, C = node_latent.shape
    assert members == 1
    pts = point_skip.shape[0]
    H = w_in.shape[1]
    V = truth.shape[0]
    E = lax.axis_size("ens")
    S = lax.axis_size("space")
    Z = S // 2
    R = nodes // 8
    VP = 16
    T = min(512, pts // 2)
    tiles = pts // T
    table_len = nodes + 2 * R
    half = C // 2
    rows_b = half // E
    rows_c = rows_b // Z if rows_b % (16 * Z) == 0 else rows_b
    vmem = pl.BlockSpec(memory_space=pltpu.VMEM)
    dma = pltpu.SemaphoreType.DMA
    node_grad, gw, small = pl.pallas_call(
        functools.partial(kernel, (E, S, T, R)),
        out_shape=(
            jax.ShapeDtypeStruct((nodes, C), F32),
            jax.ShapeDtypeStruct((C, H), BF16),
            jax.ShapeDtypeStruct((VP, H), F32),
        ),
        in_specs=[vmem, pl.BlockSpec(memory_space=pl.ANY)] + [vmem] * 7,
        out_specs=(vmem, vmem, vmem),
        scratch_shapes=[
            pltpu.VMEM((pts, C), BF16),
            pltpu.VMEM((2 * table_len, C), BF16),
            pltpu.VMEM((C, 2 * table_len), BF16),
            pltpu.VMEM((2 * table_len, pts), BF16),
            pltpu.VMEM((H, C), BF16),
            pltpu.VMEM((C, pts), BF16),
            pltpu.VMEM((H, pts), BF16),
            pltpu.VMEM((H, pts), F32),
            pltpu.VMEM((H, pts), BF16),
            pltpu.VMEM((tiles, V, T), F32),
            pltpu.VMEM((tiles, E - 1, V, T), F32),
            pltpu.VMEM((VP, H), F32),
            pltpu.VMEM((VP, pts), F32),
            pltpu.VMEM((H, 128), F32),
            pltpu.VMEM((H, 128), F32),
            pltpu.VMEM((VP, T), F32),
            pltpu.VMEM((VP, T), F32),
            pltpu.VMEM((table_len, C), F32),
            pltpu.VMEM((2, R, C), BF16),
            pltpu.VMEM((2, R, C), BF16),
            pltpu.VMEM((half, H), BF16),
            pltpu.VMEM((half, H), F32),
            pltpu.VMEM((half, H), BF16),
            pltpu.VMEM((half, H), BF16),
            pltpu.VMEM((rows_b, H), F32),
            pltpu.VMEM((E - 1, rows_b, H), BF16),
            pltpu.VMEM((rows_b, H), BF16),
            pltpu.VMEM((Z - 1, rows_c, H), BF16),
            pltpu.VMEM((C, H), BF16),
            pltpu.VMEM((VP, H), F32),
            pltpu.VMEM((VP, H), F32),
            pltpu.VMEM((E - 1, VP, H), F32),
            pltpu.VMEM((Z - 1, VP, H), F32),
            dma, dma((2,)), dma((2,)),
            dma((tiles, E - 1)), dma((tiles, E - 1)),
            dma((2,)), dma((2,)),
            dma, dma,
            dma((E - 1,)), dma((E - 1,)),
            dma((Z - 1,)), dma((Z - 1,)),
            dma((Z - 1,)), dma((Z - 1,)),
            dma((E - 1,)), dma((E - 1,)),
            dma((E,)), dma((E,)),
            dma, dma,
            dma((E - 1,)), dma((E - 1,)),
            dma((Z - 1,)), dma((Z - 1,)),
        ],
        compiler_params=pltpu.CompilerParams(
            collective_id=0, has_side_effects=True, vmem_limit_bytes=52 * 2**20
        ),
        cost_estimate=pl.CostEstimate(flops=8 * 10**9, bytes_accessed=5 * 10**6, transcendentals=2 * 10**6),
    )(
        node_latent[0], point_skip, edge_index, edge_weight, w_in, b_in[None], readout_matrix,
        jnp.pad(output_bias, (0, 128 - V))[None], truth,
    )
    points = pts * S
    scale = 1.0 / math.sqrt(E * points)
    loss = small[V + 1, VP] / (points * V)
    return (
        loss, node_grad[None], gw.astype(F32) * scale, small[V] * scale,
        small[:V] * scale, small[V + 1, :V] * scale,
    )


def solution(mesh):
    return jax.shard_map(
        per_device,
        mesh=mesh,
        in_specs=(
            P("ens", "space", None), P("space", None), P(None, "space"), P(None, "space"),
            P(), P(), P(), P(), P(None, "space"),
        ),
        out_specs=(P(), P("ens", "space", None), P(), P(), P(), P()),
        check_vma=False,
    )
```

time: 192 us -> 52.9 us (0.28)
  waiting for transfers between devices: 72.3 us -> 0 us
  blocking collectives: 55.4 us -> 0 us
  Pallas kernels: 0 us -> 40.4 us
  matrix products: 28.6 us -> 0 us
  between operations: 17.4 us -> 2.43 us
  starting transfers between devices: 8 us -> 0 us
    psum x1 -> x0, waiting for transfers between devices: 72.3 us -> none  [per_device(): lax.psum((gw_in, gb_in, readout_matrix_adjoint, readout_offset_adjoint, a...]
    psum x1 -> x0, blocking collectives: 43.6 us -> none  [per_device(): lax.psum((gw_in, gb_in, readout_matrix_adjoint, readout_offset_adjoint, a...]
    pallas_call x0 -> x1, Pallas kernels: none -> 40.4 us  [per_device(): pl.pallas_call(functools.partial(kernel, (E, S, T, R)), out_shape=(jax.Sh...]
    dot_general x8 -> x0, matrix products: 28.6 us -> none  [the longest x1 10.4 us: per_device(): jnp.einsum('pq,mpc->mqc', edge_table, d_features, precision=lax.Precision...]
    all_gather x1 -> x0, blocking collectives: 11.9 us -> none  [per_device(): lax.all_gather(modelled_state_values, 'ens', axis=0, tiled=True)]
    ppermute x4 -> x0, starting transfers between devices: 7.96 us -> none  [the longest x2 4.33 us: shifted(): lax.ppermute(value, axis, [(source, source + steps) for source in range(i...]
    mul x2 -> x4, other arithmetic: 0.01 us -> 2.83 us  [the longest x1 1.11 us: per_device(): gw.astype(F32) * scale]
    slice x5 -> x1, local copies, waits for them, and re-layouts: 2.7 us -> 0.58 us  [per_device(): loss = small[V + 1, VP] / (points * V)]
  transfers between devices with their start and end apart: 5 -> 0, of which waited for: 1 -> 0; matrix products, arithmetic and copies ran while one was open for 8% -> 0% of each run, Pallas kernels for 0% -> 0%
where the time goes in v1:
time: 52.9 us; the launch traced here: 52.5 us
  Pallas kernels  40.4 us (76%)
  local copies, waits for them, and re-layouts  6.8 us (13%)
  other arithmetic  2.83 us (5%)
  between operations  2.43 us (5%)
    pallas_call x1, Pallas kernels, per_device(): pl.pallas_call(functools.partial(kernel, (E, S, T, R)), out_shape=(jax.Sh...  40.4 us
    unnamed x13, local copies, waits for them, and re-layouts  5.56 us
    mul x1, other arithmetic, per_device(): gw.astype(F32) * scale  1.11 us

profile of v1, /device:TPU:0, one launch (start us, length us, event | category | flops | bytes accessed | tf_op | source)
XLA Modules:
  0.0 52.5 jit_solution(14620459696412565379)
XLA Ops:
  0.6 0.7 %pad_bitcast_fusion.bias = f32[1,128]{1,0:T(1,128)S(1)} fusion(f32[10]{0:T(128)} %param.16), kind=kLoop, calls=%fused_computation.4 | loop fusion | bytes 552 | tf_op jit(solution)/shard_map/broadcast_in_dim | solution.py:457
  1.3 0.0 copy-start
  1.3 0.9 %copy-done = bf16[1,256,512]{2,1,0:T(8,128)(2,1)S(1)} copy-done((bf16[1,256,512]{2,1,0:T(8,128)(2,1)S(1)}, bf16[1,256,512]{2,1,0:T(8,128)(2,1)}, u32[]{:S(2)}) %copy-start) | copy-done | bytes 262168
  2.2 0.0 copy-start.1
  2.2 0.9 %copy-done.1 = f32[10,2048]{1,0:T(8,128)S(1)} copy-done((f32[10,2048]{1,0:T(8,128)S(1)}, f32[10,2048]{1,0:T(8,128)}, u32[]{:S(2)}) %copy-start.1) | copy-done | bytes 81944
  3.1 0.0 copy-start.2
  3.1 0.8 %copy-done.2 = s32[3,2048]{1,0:T(4,128)S(1)} copy-done((s32[3,2048]{1,0:T(4,128)S(1)}, s32[3,2048]{1,0:T(4,128)}, u32[]{:S(2)}) %copy-start.2) | copy-done | bytes 24600
  3.9 0.0 copy-start.3
  3.9 0.8 %copy-done.3 = f32[3,2048]{1,0:T(4,128)S(1)} copy-done((f32[3,2048]{1,0:T(4,128)S(1)}, f32[3,2048]{1,0:T(4,128)}, u32[]{:S(2)}) %copy-start.3) | copy-done | bytes 24600
  4.7 0.0 copy-start.4
  4.7 0.7 %copy-done.4 = bf16[10,512]{1,0:T(8,128)(2,1)S(1)} copy-done((bf16[10,512]{1,0:T(8,128)(2,1)S(1)}, bf16[10,512]{1,0:T(8,128)(2,1)}, u32[]{:S(2)}) %copy-start.4) | copy-done | bytes 10264
  5.4 0.0 copy-start.5
  5.4 0.7 %copy-done.5 = f32[512]{0:T(512)S(1)} copy-done((f32[512]{0:T(512)S(1)}, f32[512]{0:T(512)}, u32[]{:S(2)}) %copy-start.5) | copy-done | bytes 2072
  6.1 40.4 %shard_map.136 = (f32[256,512]{1,0:T(8,128)S(1)}, bf16[512,512]{1,0:T(8,128)(2,1)S(1)}, f32[16,512]{1,0:T(8,128)S(1)}) custom-call(bf16[256,512]{1,0:T(8,128)(2,1)S(1)} %bitcast.10, bf16[2048,512]{1,0:T(8,128)(2,1)} %skip_hbm.1, s32[3,2048]{1,0:T(4,128)S(1)} %copy-done.2, f32[3,2048]{1,0:T(4,128)S(1)} %copy-done.3, bf16[512,512]{1,0:T(8,128)(2,1)} %w_in.1, ...), custom_call_target="tpu_custom_call" | custom-call | flops 8000000000 | bytes 5000000 | tf_op jit(solution)/shard_map/pallas_call | solution.py:395
  46.5 0.6 %slice.12 = f32[1,1]{1,0:T(1,128)} slice(f32[16,512]{1,0:T(8,128)S(1)} %get-tuple-element.9), slice={[11:12], [16:17]} | slice | bytes 8 | tf_op jit(solution)/shard_map/slice | solution.py:461
  47.7 1.1 %convert_multiply_fusion = f32[512,512]{1,0:T(8,128)} fusion(bf16[512,512]{1,0:T(8,128)(2,1)S(1)} %get-tuple-element.11), kind=kLoop, calls=%fused_computation | loop fusion | flops 524288 | bytes 1572864 | tf_op jit(solution)/shard_map/mul | solution.py:463
  48.9 0.6 %slice_multiply_fusion.1 = f32[1,512]{1,0:T(1,128)} fusion(f32[16,512]{1,0:T(8,128)S(1)} %get-tuple-element.9), kind=kLoop, calls=%fused_computation.2 | loop fusion | flops 512 | bytes 4096 | tf_op jit(solution)/shard_map/mul | solution.py:463
  49.4 0.6 %slice_multiply_fusion = f32[10,512]{1,0:T(8,128)} fusion(f32[16,512]{1,0:T(8,128)S(1)} %get-tuple-element.9), kind=kLoop, calls=%fused_computation.1 | loop fusion | flops 5120 | bytes 40960 | tf_op jit(solution)/shard_map/mul | solution.py:464
  50.1 0.5 multiply_bitcast_fusion
  50.6 0.8 %copy.16 = f32[1,256,512]{2,1,0:T(8,128)} copy(f32[1,256,512]{2,1,0:T(8,128)S(1)} %bitcast.9) | data formatting | bytes 1048576
Async XLA Ops:
  1.3 0.9 %copy-start = (bf16[1,256,512]{2,1,0:T(8,128)(2,1)S(1)}, bf16[1,256,512]{2,1,0:T(8,128)(2,1)}, u32[]{:S(2)}) copy-start(bf16[1,256,512]{2,1,0:T(8,128)(2,1)} %param.9) | copy-start | bytes 786436
  2.2 0.9 %copy-start.1 = (f32[10,2048]{1,0:T(8,128)S(1)}, f32[10,2048]{1,0:T(8,128)}, u32[]{:S(2)}) copy-start(f32[10,2048]{1,0:T(8,128)} %truth.1) | copy-start | bytes 245764
  3.1 0.8 %copy-start.2 = (s32[3,2048]{1,0:T(4,128)S(1)}, s32[3,2048]{1,0:T(4,128)}, u32[]{:S(2)}) copy-start(s32[3,2048]{1,0:T(4,128)} %index.1) | copy-start | bytes 73732
  3.9 0.8 %copy-start.3 = (f32[3,2048]{1,0:T(4,128)S(1)}, f32[3,2048]{1,0:T(4,128)}, u32[]{:S(2)}) copy-start(f32[3,2048]{1,0:T(4,128)} %weight.1) | copy-start | bytes 73732
  4.7 0.7 %copy-start.4 = (bf16[10,512]{1,0:T(8,128)(2,1)S(1)}, bf16[10,512]{1,0:T(8,128)(2,1)}, u32[]{:S(2)}) copy-start(bf16[10,512]{1,0:T(8,128)(2,1)} %readout.1) | copy-start | bytes 30724
  5.4 0.7 %copy-start.5 = (f32[512]{0:T(512)S(1)}, f32[512]{0:T(512)}, u32[]{:S(2)}) copy-start(f32[512]{0:T(512)} %param.14) | copy-start | bytes 6148

commit v2 on v1

v2 whole, which is shorter than its diff:
```python
import functools
import math

import jax
import jax.numpy as jnp
from jax import lax
from jax.experimental import pallas as pl
from jax.experimental.pallas import tpu as pltpu
from jax.sharding import PartitionSpec as P

UNBIASING = 0.95
F32 = jnp.float32
BF16 = jnp.bfloat16
NT = (((1,), (1,)), ((), ()))


def dot(a, b):
    return jnp.dot(a, b, preferred_element_type=F32)


def dot_nt(a, b):
    return lax.dot_general(a, b, NT, preferred_element_type=F32)


def sign(x):
    return jnp.where(x > 0, 1.0, 0.0) - jnp.where(x < 0, 1.0, 0.0)


def kernel(
    cfg,
    latent_hbm, skip_hbm, index_hbm, weight_hbm, w_in_hbm, b_in_hbm, readout_hbm, bias_hbm, truth_hbm,
    node_hbm, gw_hbm, small_hbm,
    latent, skip, index, weight, w_in, b_in, readout, bias, truth, ext, ext_t, table, w_t, feat, hid, slope, dpre, fc, fc_in,
    ro_pad, truth_pad, b_col, acc_bin, acc_bout, acc_loss, node_grad,
    rim_send, rim_recv, gw, gw_send, sum_a, recv_a, send_b, sum_b, recv_b, send_c, recv_c, gout,
    small, small_send, small_a, small_b, small_c,
    local_sem, out_sem, halo_s, halo_r, fc_s, fc_r, rim_s, rim_r, a_s, a_r, b_s, b_r, c_s, c_r,
    gc_s, gc_r, gb_s, gb_r, ga_s, ga_r, sa_s, sa_r, sb_s, sb_r, sc_s, sc_r,
):
    E, S, T, R, Q = cfg
    Z = S // 2
    nodes, C = latent.shape
    H = w_in.shape[1]
    pts = skip.shape[0]
    K = index.shape[0]
    V = readout.shape[0]
    VP = ro_pad.shape[0]
    tiles = pts // T
    table_len = nodes + 2 * R
    e = lax.axis_index("ens")
    s = lax.axis_index("space")
    c = lax.rem(s, 2)
    z = lax.div(s, 2)
    partner = s + 1 - 2 * c
    far = s - 1 + 2 * c
    has_far = jnp.logical_and(far >= 0, far < S)

    loads = [
        pltpu.make_async_copy(src, dst, local_sem.at[i])
        for i, (src, dst) in enumerate((
            (index_hbm, index), (weight_hbm, weight), (latent_hbm, latent), (w_in_hbm, w_in), (b_in_hbm, b_in),
            (readout_hbm, readout), (bias_hbm, bias), (truth_hbm, truth), (skip_hbm, skip),
        ))
    ]
    for load in loads:
        load.start()

    barrier = pltpu.get_barrier_semaphore()

    def greet(dev):
        pl.semaphore_signal(barrier, inc=1, device_id=dev, device_id_type=pl.DeviceIdType.MESH)

    def ens_peer(d):
        return lax.rem(e + d, E)

    def z_peer(d):
        return lax.rem(z + d, Z)

    greet((e, partner))
    for d in range(1, E):
        greet((ens_peer(d), s))
    for d in range(1, Z):
        greet((e, 2 * z_peer(d) + c))

    @pl.when(has_far)
    def _():
        greet((e, far))

    def remote(src, dst, ss, rs, dev):
        return pltpu.make_async_remote_copy(
            src_ref=src, dst_ref=dst, send_sem=ss, recv_sem=rs,
            device_id=dev, device_id_type=pl.DeviceIdType.MESH,
        )

    for load in loads[:-1]:
        load.wait()
    ext[pl.ds(R, nodes)] = latent[...]
    ext[pl.ds(table_len + R, nodes)] = latent[...]
    w_t[...] = jnp.transpose(w_in[...])
    b_col[...] = jnp.transpose(jnp.broadcast_to(b_in[...], (128, H)))
    ro_pad[...] = jnp.zeros_like(ro_pad)
    ro_pad[pl.ds(0, V)] = readout[...].astype(F32)
    truth_pad[...] = jnp.zeros_like(truth_pad)
    truth_pad[pl.ds(0, V)] = truth[...]
    acc_bin[...] = jnp.zeros_like(acc_bin)
    acc_bout[...] = jnp.zeros_like(acc_bout)
    acc_loss[...] = jnp.zeros_like(acc_loss)
    small[...] = jnp.zeros_like(small)
    ro = ro_pad[...].astype(BF16)
    ro_t = jnp.transpose(ro_pad[...]).astype(BF16)
    row_v = lax.broadcasted_iota(jnp.int32, (VP, V), 0)
    lane_v = lax.broadcasted_iota(jnp.int32, (VP, V), 1)
    bias_col = jnp.sum(
        jnp.where(row_v == lane_v, jnp.broadcast_to(bias[...], (VP, V)), 0.0), axis=1, keepdims=True
    )

    def lanes(i):
        return pl.ds(pl.multiple_of(i * T, T), T)

    def make_table(i, carry):
        slot = lax.broadcasted_iota(jnp.int32, (table_len, T), 0)
        total = jnp.zeros((table_len, T), F32)
        for k in range(K):
            total = total + jnp.where(slot == index[pl.ds(k, 1), lanes(i)], weight[pl.ds(k, 1), lanes(i)], 0.0)
        high = total.astype(BF16)
        table[pl.ds(0, table_len), lanes(i)] = high
        table[pl.ds(table_len, table_len), lanes(i)] = (total - high.astype(F32)).astype(BF16)
        return carry

    lax.fori_loop(0, tiles // 2, make_table, 0)

    pl.semaphore_wait(barrier, E + Z - 1 + has_far.astype(jnp.int32))

    up = remote(latent.at[pl.ds(nodes - R, R)], ext.at[pl.ds(0, R)], halo_s.at[0], halo_r.at[0], (e, s + 1))
    down = remote(latent.at[pl.ds(0, R)], ext.at[pl.ds(R + nodes, R)], halo_s.at[1], halo_r.at[1], (e, s - 1))

    @pl.when(s < S - 1)
    def _():
        up.start()

    @pl.when(s > 0)
    def _():
        down.start()

    @pl.when(s == 0)
    def _():
        ext[pl.ds(0, R)] = jnp.zeros((R, C), BF16)

    @pl.when(s == S - 1)
    def _():
        ext[pl.ds(R + nodes, R)] = jnp.zeros((R, C), BF16)

    lax.fori_loop(tiles // 2, tiles, make_table, 0)
    loads[-1].wait()

    @pl.when(s < S - 1)
    def _():
        down.wait_recv()

    @pl.when(s > 0)
    def _():
        up.wait_recv()

    ext[pl.ds(table_len, R)] = ext[pl.ds(0, R)]
    ext[pl.ds(table_len + R + nodes, R)] = ext[pl.ds(R + nodes, R)]
    ext_t[...] = jnp.transpose(ext[...])

    units = 20.0 * E * (E - 1)
    from_truth = 20.0 * (E - 1)
    from_pair = 20.0 * UNBIASING

    def fc_copy(i, d):
        return remote(fc.at[i], fc_in.at[i, d - 1], fc_s.at[i, d - 1], fc_r.at[i, d - 1], (ens_peer(d), s))

    def forward(i, carry):
        at = lanes(i)
        skip_t = jnp.transpose(skip[at, :]).astype(F32)
        f = (skip_t + dot(ext_t[...], table[:, at])).astype(BF16)
        feat[:, at] = f
        col = b_col[...]
        pre = dot(w_t[...], f) + jnp.concatenate([col] * (T // 128), axis=1)
        sig = 1.0 / (1.0 + jnp.exp(-pre))
        h = pre * sig
        slope[:, at] = (sig + h * (1.0 - sig)) * (1.0 / units)
        hb = h.astype(BF16)
        hid[:, at] = hb
        fc[i] = (dot(ro, hb) + bias_col)[:V]
        for d in range(1, E):
            fc_copy(i, d).start()
        return carry

    lax.fori_loop(0, tiles, forward, 0)

    def backward(i, carry):
        at = lanes(i)
        for d in range(1, E):
            fc_copy(i, d).wait_recv()
        own = fc[i]
        gap = own - truth_pad[pl.ds(0, V), at]
        pairs = jnp.zeros_like(own)
        spread = jnp.zeros_like(own)
        for d in range(1, E):
            diff = own - fc_in[i, d - 1]
            pairs = pairs + sign(diff)
            spread = spread + jnp.abs(diff)
        adj = from_truth * sign(gap) - from_pair * pairs
        acc_bout[pl.ds(0, V)] += adj
        acc_loss[pl.ds(0, V)] += jnp.abs(gap) * (1.0 / E) - spread * (UNBIASING / (2.0 * E * (E - 1)))
        truth_pad[pl.ds(0, V), at] = adj
        g = truth_pad[:, at].astype(BF16)
        small[...] += dot_nt(g, hid[:, at])
        dp = (dot(ro_t, g) * slope[:, at]).astype(BF16)
        dpre[:, at] = dp
        dp32 = dp.astype(F32)
        part = dp32[:, 0:128]
        for j in range(1, T // 128):
            part = part + dp32[:, j * 128:(j + 1) * 128]
        acc_bin[...] += part
        return carry

    lax.fori_loop(0, tiles - 1, backward, 0)
    done = (tiles - 1) * T
    gw[...] = dot_nt(feat[:, :done], dpre[:, :done])
    lax.fori_loop(tiles - 1, tiles, backward, 0)

    row = lax.broadcasted_iota(jnp.int32, (VP, H), 0)
    lane = lax.broadcasted_iota(jnp.int32, (VP, H), 1)
    gb_in = jnp.sum(jnp.transpose(acc_bin[...]), axis=0, keepdims=True)
    gb_col = jnp.sum(acc_bout[...], axis=1, keepdims=True)
    loss_col = jnp.sum(acc_loss[...], axis=1, keepdims=True)
    tail = jnp.sum(
        jnp.where(lane == row, gb_col * (1.0 / units), 0.0) + jnp.where(lane == VP, loss_col, 0.0),
        axis=0, keepdims=True,
    )
    first = small[...] * (1.0 / units)
    first = first + jnp.where(row == V, gb_in, 0.0) + jnp.where(row == V + 1, tail, 0.0)
    small[...] = first

    def pack_small():
        value = small[...]
        high = value.astype(BF16).astype(F32)
        low = jnp.broadcast_to((value - high)[V + 1:V + 2], (VP, H))
        small_send[...] = jnp.where(row == V + 2, low, high).astype(BF16)

    def add_small(*terms):
        total = small[...]
        for term in terms:
            total = total + term.astype(F32)
        low = jnp.broadcast_to(total[V + 2:V + 3], (VP, H))
        small[...] = jnp.where(row == V + 1, total + low, jnp.where(row == V + 2, 0.0, total))

    pack_small()
    copy_sa = remote(small_send, small_a, sa_s, sa_r, (e, partner))
    copy_sa.start()

    half = C // 2
    cols = H // Q
    rows_b = half // E
    scatter_c = rows_b % (16 * Z) == 0
    rows_c = rows_b // Z if scatter_c else rows_b
    theirs = pl.multiple_of((1 - c) * half, half)
    mine = pl.multiple_of(c * half, half)

    def last_part(rows, q):
        at = pl.ds(q * cols, cols)
        return gw[pl.ds(rows, half), at] + dot_nt(feat[pl.ds(rows, half), done:], dpre[at, done:])

    copies_a = []
    for q in range(Q):
        gw_send[q] = last_part(theirs, q).astype(BF16)
        copy = remote(gw_send.at[q], recv_a.at[q], a_s.at[q], a_r.at[q], (e, partner))
        copy.start()
        copies_a.append(copy)

    copy_sa.wait()
    add_small(small_a[...])
    pack_small()
    copies_sb = [remote(small_send, small_b.at[d - 1], sb_s.at[d - 1], sb_r.at[d - 1], (ens_peer(d), s)) for d in range(1, E)]
    for copy in copies_sb:
        copy.start()

    copies_b = []
    for q in range(Q):
        own = last_part(mine, q)
        copies_a[q].wait()
        own = own + recv_a[q].astype(F32)
        sum_a[q] = own
        send_b[q] = own.astype(BF16)
        parts = [
            remote(
                send_b.at[q, pl.ds(pl.multiple_of(ens_peer(d) * rows_b, rows_b), rows_b)],
                recv_b.at[q, d - 1], b_s.at[q, d - 1], b_r.at[q, d - 1], (ens_peer(d), s),
            )
            for d in range(1, E)
        ]
        for copy in parts:
            copy.start()
        copies_b.append(parts)

    node_grad[...] = jnp.zeros_like(node_grad)
    wide = pts // 2

    def spread_back(i):
        at = pl.ds(i * wide, wide)
        df = dot(w_in[...], dpre[:, at]).astype(BF16)
        node_grad[...] += dot_nt(table[pl.ds(0, table_len), at], df)

    spread_back(0)
    for copy in copies_sb:
        copy.wait()
    add_small(*[small_b[d - 1] for d in range(1, E)])
    pack_small()
    copies_sc = [remote(small_send, small_c.at[d - 1], sc_s.at[d - 1], sc_r.at[d - 1], (e, 2 * z_peer(d) + c)) for d in range(1, Z)]
    for copy in copies_sc:
        copy.start()

    def stage_c(q):
        for copy in copies_b[q]:
            copy.wait()
        total = sum_a[q, pl.ds(pl.multiple_of(e * rows_b, rows_b), rows_b)]
        for d in range(1, E):
            total = total + recv_b[q, d - 1].astype(F32)
        sum_b[q] = total
        send_c[q] = total.astype(BF16)
        parts = []
        for d in range(1, Z):
            if scatter_c:
                src = send_c.at[q, pl.ds(pl.multiple_of(z_peer(d) * rows_c, rows_c), rows_c)]
            else:
                src = send_c.at[q]
            parts.append(remote(src, recv_c.at[q, d - 1], c_s.at[q, d - 1], c_r.at[q, d - 1], (e, 2 * z_peer(d) + c)))
        for copy in parts:
            copy.start()
        return parts

    copies_c = [stage_c(0)]
    spread_back(1)
    for q in range(1, Q):
        copies_c.append(stage_c(q))

    rim_send[0] = node_grad[pl.ds(R + nodes, R)].astype(BF16)
    rim_send[1] = node_grad[pl.ds(0, R)].astype(BF16)
    rim_up = remote(rim_send.at[0], rim_recv.at[0], rim_s.at[0], rim_r.at[0], (e, s + 1))
    rim_down = remote(rim_send.at[1], rim_recv.at[1], rim_s.at[1], rim_r.at[1], (e, s - 1))

    @pl.when(s < S - 1)
    def _():
        rim_up.start()

    @pl.when(s > 0)
    def _():
        rim_down.start()

    base_b = pl.multiple_of(c * half + e * rows_b, rows_b)
    base_c = pl.multiple_of(base_b + z * rows_c, rows_c) if scatter_c else base_b
    copies_gc = []
    for q in range(Q):
        for copy in copies_c[q]:
            copy.wait()
        if scatter_c:
            total = sum_b[q, pl.ds(pl.multiple_of(z * rows_c, rows_c), rows_c)]
        else:
            total = sum_b[q]
        for d in range(1, Z):
            total = total + recv_c[q, d - 1].astype(F32)
        gout[q, pl.ds(base_c, rows_c)] = total.astype(BF16)
        parts = []
        if scatter_c:
            piece = gout.at[q, pl.ds(base_c, rows_c)]
            parts = [remote(piece, piece, gc_s.at[q, d - 1], gc_r.at[q, d - 1], (e, 2 * z_peer(d) + c)) for d in range(1, Z)]
            for copy in parts:
                copy.start()
        copies_gc.append(parts)

    def to_partner(q, d):
        at = pl.multiple_of(c * half + lax.rem(e + E - d, E) * rows_b, rows_b)
        piece = gout.at[q, pl.ds(at, rows_b)]
        return remote(piece, piece, ga_s.at[q, d], ga_r.at[q, d], (e, partner))

    copies_gb = []
    for q in range(Q):
        for copy in copies_gc[q]:
            copy.wait()
        piece = gout.at[q, pl.ds(base_b, rows_b)]
        parts = [remote(piece, piece, gb_s.at[q, d - 1], gb_r.at[q, d - 1], (ens_peer(d), s)) for d in range(1, E)]
        for copy in parts:
            copy.start()
        to_partner(q, 0).start()
        copies_gb.append(parts)

    @pl.when(s > 0)
    def _():
        rim_up.wait_recv()
        node_grad[pl.ds(R, R)] += rim_recv[0].astype(F32)
        rim_down.wait_send()
        down.wait_send()

    @pl.when(s < S - 1)
    def _():
        rim_down.wait_recv()
        node_grad[pl.ds(nodes, R)] += rim_recv[1].astype(F32)
        rim_up.wait_send()
        up.wait_send()

    stores = [pltpu.make_async_copy(node_grad.at[pl.ds(R, nodes)], node_hbm, out_sem.at[0])]
    stores[0].start()
    for copy in copies_sc:
        copy.wait()
    add_small(*[small_c[d - 1] for d in range(1, Z)])
    stores.append(pltpu.make_async_copy(small, small_hbm, out_sem.at[1]))
    stores[1].start()

    def drain(i, carry):
        for d in range(1, E):
            fc_copy(i, d).wait_send()
        return carry

    lax.fori_loop(0, tiles, drain, 0)
    for q in range(Q):
        for d in range(1, E):
            copies_gb[q][d - 1].wait_recv()
            to_partner(q, d).start()
    for q in range(Q):
        for copy in copies_gb[q]:
            copy.wait_send()
        for d in range(E):
            to_partner(q, d).wait()
    stores.append(pltpu.make_async_copy(gout, gw_hbm, out_sem.at[2]))
    stores[2].start()
    for store in stores:
        store.wait()


def finish(
    scale, loss_scale, V, lane,
    node_in, gw_in, small_in, loss_hbm, node_hbm, gw_hbm, b_in_hbm, w_out_hbm, b_out_hbm,
    gw, small, loss, gw_f, b_in, w_out, b_out, sems,
):
    Q, _, cols = gw.shape
    loads = [pltpu.make_async_copy(gw_in.at[q], gw.at[q], sems.at[7 + q]) for q in range(Q)]
    loads.append(pltpu.make_async_copy(small_in, small, sems.at[7 + Q]))
    for load in loads:
        load.start()
    copies = [pltpu.make_async_copy(node_in, node_hbm, sems.at[0])]
    copies[0].start()
    for q in range(Q):
        loads[q].wait()
        at = pl.ds(q * cols, cols)
        gw_f[:, at] = gw[q].astype(F32) * scale
        copies.append(pltpu.make_async_copy(gw_f.at[:, at], gw_hbm.at[:, at], sems.at[1 + q]))
        copies[-1].start()
    loads[Q].wait()
    loss[...] = small[V + 1:V + 2, lane:lane + 1] * loss_scale
    b_in[...] = small[V:V + 1, :] * scale
    w_out[...] = small[:V, :] * scale
    b_out[...] = small[V + 1:V + 2, :V] * scale
    for i, (src, dst) in enumerate(((loss, loss_hbm), (b_in, b_in_hbm), (w_out, w_out_hbm), (b_out, b_out_hbm))):
        copies.append(pltpu.make_async_copy(src, dst, sems.at[3 + i]))
        copies[-1].start()
    for copy in copies:
        copy.wait()


def per_device(
    node_latent, point_skip, edge_index, edge_weight, w_in, b_in, readout_matrix, output_bias, truth
):
    members, nodes, C = node_latent.shape
    assert members == 1
    pts = point_skip.shape[0]
    H = w_in.shape[1]
    V = truth.shape[0]
    E = lax.axis_size("ens")
    S = lax.axis_size("space")
    Z = S // 2
    R = nodes // 8
    VP = 16
    Q = 2
    cols = H // Q
    K = edge_index.shape[0]
    T = min(512, pts // 2)
    tiles = pts // T
    table_len = nodes + 2 * R
    half = C // 2
    rows_b = half // E
    rows_c = rows_b // Z if rows_b % (16 * Z) == 0 else rows_b
    hbm = pl.BlockSpec(memory_space=pltpu.HBM)
    dma = pltpu.SemaphoreType.DMA
    node_grad, gw, small = pl.pallas_call(
        functools.partial(kernel, (E, S, T, R, Q)),
        out_shape=(
            jax.ShapeDtypeStruct((nodes, C), F32),
            jax.ShapeDtypeStruct((Q, C, cols), BF16),
            jax.ShapeDtypeStruct((VP, H), F32),
        ),
        in_specs=[hbm] * 9,
        out_specs=(hbm, hbm, hbm),
        scratch_shapes=[
            pltpu.VMEM((nodes, C), BF16),
            pltpu.VMEM((pts, C), BF16),
            pltpu.VMEM((K, pts), jnp.int32),
            pltpu.VMEM((K, pts), F32),
            pltpu.VMEM((C, H), BF16),
            pltpu.VMEM((1, H), F32),
            pltpu.VMEM((V, H), BF16),
            pltpu.VMEM((1, V), F32),
            pltpu.VMEM((V, pts), F32),
            pltpu.VMEM((2 * table_len, C), BF16),
            pltpu.VMEM((C, 2 * table_len), BF16),
            pltpu.VMEM((2 * table_len, pts), BF16),
            pltpu.VMEM((H, C), BF16),
            pltpu.VMEM((C, pts), BF16),
            pltpu.VMEM((H, pts), BF16),
            pltpu.VMEM((H, pts), F32),
            pltpu.VMEM((H, pts), BF16),
            pltpu.VMEM((tiles, V, T), F32),
            pltpu.VMEM((tiles, E - 1, V, T), F32),
            pltpu.VMEM((VP, H), F32),
            pltpu.VMEM((VP, pts), F32),
            pltpu.VMEM((H, 128), F32),
            pltpu.VMEM((H, 128), F32),
            pltpu.VMEM((VP, T), F32),
            pltpu.VMEM((VP, T), F32),
            pltpu.VMEM((table_len, C), F32),
            pltpu.VMEM((2, R, C), BF16),
            pltpu.VMEM((2, R, C), BF16),
            pltpu.VMEM((C, H), F32),
            pltpu.VMEM((Q, half, cols), BF16),
            pltpu.VMEM((Q, half, cols), F32),
            pltpu.VMEM((Q, half, cols), BF16),
            pltpu.VMEM((Q, half, cols), BF16),
            pltpu.VMEM((Q, rows_b, cols), F32),
            pltpu.VMEM((Q, E - 1, rows_b, cols), BF16),
            pltpu.VMEM((Q, rows_b, cols), BF16),
            pltpu.VMEM((Q, Z - 1, rows_c, cols), BF16),
            pltpu.VMEM((Q, C, cols), BF16),
            pltpu.VMEM((VP, H), F32),
            pltpu.VMEM((VP, H), BF16),
            pltpu.VMEM((VP, H), BF16),
            pltpu.VMEM((E - 1, VP, H), BF16),
            pltpu.VMEM((Z - 1, VP, H), BF16),
            dma((9,)), dma((3,)), dma((2,)), dma((2,)),
            dma((tiles, E - 1)), dma((tiles, E - 1)),
            dma((2,)), dma((2,)),
            dma((Q,)), dma((Q,)),
            dma((Q, E - 1)), dma((Q, E - 1)),
            dma((Q, Z - 1)), dma((Q, Z - 1)),
            dma((Q, Z - 1)), dma((Q, Z - 1)),
            dma((Q, E - 1)), dma((Q, E - 1)),
            dma((Q, E)), dma((Q, E)),
            dma, dma,
            dma((E - 1,)), dma((E - 1,)),
            dma((Z - 1,)), dma((Z - 1,)),
        ],
        compiler_params=pltpu.CompilerParams(
            collective_id=0, has_side_effects=True, vmem_limit_bytes=62 * 2**20
        ),
        cost_estimate=pl.CostEstimate(flops=8 * 10**9, bytes_accessed=5 * 10**6, transcendentals=2 * 10**6),
    )(
        node_latent[0], point_skip, edge_index, edge_weight, w_in, b_in[None], readout_matrix,
        output_bias[None], truth,
    )
    points = pts * S
    scale = 1.0 / math.sqrt(E * points)
    sds = jax.ShapeDtypeStruct
    loss, node_grad, gw, gb_in, gw_out, gb_out = pl.pallas_call(
        functools.partial(finish, scale, 1.0 / (points * V), V, VP),
        out_shape=(
            sds((1, 1), F32), sds((nodes, C), F32), sds((C, H), F32),
            sds((1, H), F32), sds((V, H), F32), sds((1, V), F32),
        ),
        in_specs=[hbm] * 3,
        out_specs=(hbm,) * 6,
        scratch_shapes=[
            pltpu.VMEM((Q, C, cols), BF16), pltpu.VMEM((VP, H), F32),
            pltpu.VMEM((1, 1), F32), pltpu.VMEM((C, H), F32), pltpu.VMEM((1, H), F32),
            pltpu.VMEM((V, H), F32), pltpu.VMEM((1, V), F32), dma((8 + Q,)),
        ],
        compiler_params=pltpu.CompilerParams(vmem_limit_bytes=62 * 2**20),
    )(node_grad, gw, small)
    return loss[0, 0], node_grad[None], gw, gb_in[0], gw_out, gb_out[0]


def solution(mesh):
    return jax.shard_map(
        per_device,
        mesh=mesh,
        in_specs=(
            P("ens", "space", None), P("space", None), P(None, "space"), P(None, "space"),
            P(), P(), P(), P(), P(None, "space"),
        ),
        out_specs=(P(), P("ens", "space", None), P(), P(), P(), P()),
        check_vma=False,
    )
```

time: 52.9 us -> 56.1 us (1.060)
  Pallas kernels: 40.4 us -> 55.3 us
  local copies, waits for them, and re-layouts: 6.8 us -> 0 us
  other arithmetic: 2.83 us -> 0 us
  between operations: 2.43 us -> 0.64 us
    pallas_call x1 -> x2, Pallas kernels: 40.4 us -> 55.3 us  [the longest x1 38.2 us: per_device(): pl.pallas_call(functools.partial(kernel, (E, S, T, R, Q)), out_shape=(jax...]
    unnamed x13 -> x0, local copies, waits for them, and re-layouts: 5.56 us -> none
    mul x4 -> x0, other arithmetic: 2.83 us -> none  [the longest x1 1.11 us: per_device(): gw.astype(F32) * scale]
    broadcast_in_dim x1 -> x0, local copies, waits for them, and re-layouts: 0.66 us -> none  [per_device(): jnp.pad(output_bias, (0, 128 - V))[None]]
    slice x1 -> x0, local copies, waits for them, and re-layouts: 0.58 us -> none  [per_device(): loss = small[V + 1, VP] / (points * V)]
where the time goes in v2:
time: 56.1 us; the launch traced here: 56 us
  Pallas kernels  55.3 us (99%)
  between operations  0.64 us (1%)
    pallas_call x1, Pallas kernels, per_device(): pl.pallas_call(functools.partial(kernel, (E, S, T, R, Q)), out_shape=(jax...  38.2 us
    pallas_call x1, Pallas kernels, per_device(): pl.pallas_call(functools.partial(finish, scale, 1.0 / (points * V), V, VP...  17.1 us

profile of v2, /device:TPU:0, one launch (start us, length us, event | category | flops | bytes accessed | tf_op | source)
XLA Modules:
  0.0 56.0 jit_solution(8500951391128387628)
XLA Ops:
  0.6 38.2 %shard_map.136 = (f32[256,512]{1,0:T(8,128)}, bf16[2,512,256]{2,1,0:T(8,128)(2,1)}, f32[16,512]{1,0:T(8,128)}) custom-call(bf16[256,512]{1,0:T(8,128)(2,1)} %bitcast.8, bf16[2048,512]{1,0:T(8,128)(2,1)} %skip_hbm.1, s32[3,2048]{1,0:T(4,128)} %index_hbm.1, f32[3,2048]{1,0:T(4,128)} %weight_hbm.1, bf16[512,512]{1,0:T(8,128)(2,1)} %w_in_hbm.1, ...), custom_call_target="tpu_custom_call" | custom-call | flops 8000000000 | bytes 5000000 | tf_op jit(solution)/shard_map/pallas_call | solution.py:488
  38.9 17.1 %shard_map.137 = (f32[1,1]{1,0:T(1,128)}, f32[256,512]{1,0:T(8,128)}, f32[512,512]{1,0:T(8,128)}, f32[1,512]{1,0:T(1,128)}, f32[10,512]{1,0:T(8,128)}, /*index=5*/f32[1,10]{1,0:T(1,128)}) custom-call(f32[256,512]{1,0:T(8,128)} %get-tuple-element.15.node_in, bf16[2,512,256]{2,1,0:T(8,128)(2,1)} %get-tuple-element.16.gw_in, f32[16,512]{1,0:T(8,128)} %get-tuple-element.17.small_in), custom_call_target="tpu_custom_call" | custom-call | tf_op jit(solution)/shard_map/pallas_call | solution.py:565

commit v3 on v2

--- a/solution.py
+++ b/solution.py
@@ -434,28 +434,31 @@
 def finish(
     scale, loss_scale, V, lane,
     node_in, gw_in, small_in, loss_hbm, node_hbm, gw_hbm, b_in_hbm, w_out_hbm, b_out_hbm,
-    gw, small, loss, gw_f, b_in, w_out, b_out, sems,
+    node, gw, small, loss, gw_f, b_in, w_out, b_out, sems,
 ):
     Q, _, cols = gw.shape
-    loads = [pltpu.make_async_copy(gw_in.at[q], gw.at[q], sems.at[7 + q]) for q in range(Q)]
-    loads.append(pltpu.make_async_copy(small_in, small, sems.at[7 + Q]))
+    loads = [pltpu.make_async_copy(gw_in.at[q], gw.at[q], sems.at[q]) for q in range(Q)]
+    loads.append(pltpu.make_async_copy(small_in, small, sems.at[Q]))
+    loads.append(pltpu.make_async_copy(node_in, node, sems.at[Q + 1]))
     for load in loads:
         load.start()
-    copies = [pltpu.make_async_copy(node_in, node_hbm, sems.at[0])]
-    copies[0].start()
+    copies = []
     for q in range(Q):
         loads[q].wait()
         at = pl.ds(q * cols, cols)
         gw_f[:, at] = gw[q].astype(F32) * scale
-        copies.append(pltpu.make_async_copy(gw_f.at[:, at], gw_hbm.at[:, at], sems.at[1 + q]))
+        copies.append(pltpu.make_async_copy(gw_f.at[:, at], gw_hbm.at[:, at], sems.at[Q + 2 + q]))
         copies[-1].start()
+    loads[Q + 1].wait()
+    copies.append(pltpu.make_async_copy(node, node_hbm, sems.at[2 * Q + 2]))
+    copies[-1].start()
     loads[Q].wait()
     loss[...] = small[V + 1:V + 2, lane:lane + 1] * loss_scale
     b_in[...] = small[V:V + 1, :] * scale
     w_out[...] = small[:V, :] * scale
     b_out[...] = small[V + 1:V + 2, :V] * scale
     for i, (src, dst) in enumerate(((loss, loss_hbm), (b_in, b_in_hbm), (w_out, w_out_hbm), (b_out, b_out_hbm))):
-        copies.append(pltpu.make_async_copy(src, dst, sems.at[3 + i]))
+        copies.append(pltpu.make_async_copy(src, dst, sems.at[2 * Q + 3 + i]))
         copies[-1].start()
     for copy in copies:
         copy.wait()
@@ -571,9 +574,9 @@
         in_specs=[hbm] * 3,
         out_specs=(hbm,) * 6,
         scratch_shapes=[
-            pltpu.VMEM((Q, C, cols), BF16), pltpu.VMEM((VP, H), F32),
+            pltpu.VMEM((nodes, C), F32), pltpu.VMEM((Q, C, cols), BF16), pltpu.VMEM((VP, H), F32),
             pltpu.VMEM((1, 1), F32), pltpu.VMEM((C, H), F32), pltpu.VMEM((1, H), F32),
-            pltpu.VMEM((V, H), F32), pltpu.VMEM((1, V), F32), dma((8 + Q,)),
+            pltpu.VMEM((V, H), F32), pltpu.VMEM((1, V), F32), dma((2 * Q + 7,)),
         ],
         compiler_params=pltpu.CompilerParams(vmem_limit_bytes=62 * 2**20),
     )(node_grad, gw, small)

time: 56.1 us -> 41.3 us (0.74)
  Pallas kernels: 55.3 us -> 40.5 us
    pallas_call x1, Pallas kernels: 17.1 us -> 2.23 us  [per_device(): pl.pallas_call(functools.partial(finish, scale, 1.0 / (points * V), V, VP...]
where the time goes in v3:
time: 41.3 us; the launch traced here: 41.1 us
  Pallas kernels  40.5 us (98%)
  between operations  0.64 us (2%)
    pallas_call x1, Pallas kernels, per_device(): pl.pallas_call(functools.partial(kernel, (E, S, T, R, Q)), out_shape=(jax...  38.2 us
    pallas_call x1, Pallas kernels, per_device(): pl.pallas_call(functools.partial(finish, scale, 1.0 / (points * V), V, VP...  2.23 us

profile of v3, /device:TPU:0, one launch (start us, length us, event | category | flops | bytes accessed | tf_op | source)
XLA Modules:
  0.0 41.1 jit_solution(17840893406749597661)
XLA Ops:
  0.6 38.2 %shard_map.136 = (f32[256,512]{1,0:T(8,128)}, bf16[2,512,256]{2,1,0:T(8,128)(2,1)}, f32[16,512]{1,0:T(8,128)}) custom-call(bf16[256,512]{1,0:T(8,128)(2,1)} %bitcast.8, bf16[2048,512]{1,0:T(8,128)(2,1)} %skip_hbm.1, s32[3,2048]{1,0:T(4,128)} %index_hbm.1, f32[3,2048]{1,0:T(4,128)} %weight_hbm.1, bf16[512,512]{1,0:T(8,128)(2,1)} %w_in_hbm.1, ...), custom_call_target="tpu_custom_call" | custom-call | flops 8000000000 | bytes 5000000 | tf_op jit(solution)/shard_map/pallas_call | solution.py:491
  38.9 2.2 %shard_map.137 = (f32[1,1]{1,0:T(1,128)}, f32[256,512]{1,0:T(8,128)}, f32[512,512]{1,0:T(8,128)}, f32[1,512]{1,0:T(1,128)}, f32[10,512]{1,0:T(8,128)}, /*index=5*/f32[1,10]{1,0:T(1,128)}) custom-call(f32[256,512]{1,0:T(8,128)} %get-tuple-element.15.node_in, bf16[2,512,256]{2,1,0:T(8,128)(2,1)} %get-tuple-element.16.gw_in, f32[16,512]{1,0:T(8,128)} %get-tuple-element.17.small_in), custom_call_target="tpu_custom_call" | custom-call | tf_op jit(solution)/shard_map/pallas_call | solution.py:568
